TPU v7x, 512 devices: a whole 4x8x8 slice. The times are simulated.
512 devices in a mesh: adapter: 64 (over x, y, core), tensor: 8 (over z).
Axes of the slice: x: 4, y: 8, z: 8, core: 2. Of those that a mesh axis runs over, the one named last changes fastest.
Arguments:
- tokens: bfloat16 [32768, 8192], P('adapter', 'tensor'), may hold values from -6 to 6
- token_adapter_index: int32 [32768], P('adapter'), may hold values from 0 to 127, as said below
- adapter_stored_row: int32 [128], replicated, may hold values from 0 to 127, as said below
- value_base_weight: bfloat16 [8192, 1024], P('tensor'), may hold values from -0.09375 to 0.09375
- adapter_down_maps: bfloat16 [128, 64, 8192], P('adapter', None, 'tensor'), may hold values from -0.0625 to 0.0625
- adapter_up_maps: bfloat16 [128, 64, 1024], P('adapter', None, 'tensor'), may hold values from -0.75 to 0.75
Outputs:
- values: bfloat16 [32768, 1024], P('adapter', 'tensor')
Inputs may be any that keep to these rules, and one draw needn't show every extreme that they name: adapter_stored_row is a permutation; stored row s belongs to owner s // 2. `token_adapter_index`: among the 512 tokens of each index of adapter (consecutive rows), at most 10 have adapters whose stored rows belong to one owner.
All inputs are finite; a program needn't handle non-finite values.
Results may differ from a plain program's by a relative error of at most 0.0053.
Values may be sent and summed in bfloat16 or wider, within the bound.
A program may use at most 64 MiB of HBM per device.

v0:
```python
import jax
import jax.numpy as jnp
from jax import lax
from jax.sharding import PartitionSpec as P

adapter_scale = 2.0


def base_product(tokens, value_base_weight):
    partials = jnp.dot(tokens, value_base_weight, preferred_element_type=jnp.float32)
    return lax.psum_scatter(partials, "tensor", scatter_dimension=1, tiled=True)


def local(
    tokens,
    token_adapter_index,
    adapter_stored_row,
    value_base_weight,
    adapter_down_maps,
    adapter_up_maps,
):
    rows, width = tokens.shape
    owners_count = lax.axis_size("adapter")
    resident_count = adapter_down_maps.shape[0]
    rank_columns = adapter_down_maps.shape[1]
    capacity = rows // owners_count + rows // (4 * owners_count)
    table_size = adapter_stored_row.shape[0]
    lookup = token_adapter_index[:, None] == jnp.arange(table_size, dtype=jnp.int32)[None, :]
    slot = jnp.sum(jnp.where(lookup, adapter_stored_row[None, :], 0), axis=1)
    owner = slot // resident_count
    within = slot % resident_count
    member = (owner[:, None] == jnp.arange(owners_count, dtype=jnp.int32)[None, :]).astype(
        jnp.int32
    )
    before = jnp.sum((jnp.cumsum(member, axis=0) - member) * member, axis=1)
    target = owner * capacity + before
    send_rows = jnp.zeros((owners_count * capacity, width), jnp.bfloat16).at[target].set(tokens)
    send_place = jnp.full((owners_count * capacity,), -1, jnp.int32).at[target].set(within)
    received_rows, arrived_place = (
        lax.all_to_all(
            send_rows.reshape(owners_count, capacity, width),
            "adapter",
            split_axis=0,
            concat_axis=0,
            tiled=True,
        ),
        lax.all_to_all(
            send_place.reshape(owners_count, capacity),
            "adapter",
            split_axis=0,
            concat_axis=0,
            tiled=True,
        ),
    )
    received_rows = received_rows.reshape(owners_count * capacity, width)
    arrived_place = arrived_place.reshape(owners_count * capacity)
    select = (
        arrived_place[:, None] == jnp.arange(resident_count, dtype=jnp.int32)[None, :]
    ).astype(jnp.float32)
    partial_all = jnp.einsum(
        "yn,vln->yvl", received_rows, adapter_down_maps, preferred_element_type=jnp.float32
    )
    partial_value = jnp.sum(partial_all * select[:, :, None], axis=1)
    shrunk = lax.psum(partial_value, "tensor").astype(jnp.bfloat16)
    spread_rows = (select.astype(jnp.bfloat16)[:, :, None] * shrunk[:, None, :]).reshape(
        owners_count * capacity, resident_count * rank_columns
    )
    stacked_up_maps = adapter_up_maps.reshape(
        resident_count * rank_columns, adapter_up_maps.shape[2]
    )
    adapter_update = (
        adapter_scale * jnp.dot(spread_rows, stacked_up_maps, preferred_element_type=jnp.float32)
    ).astype(jnp.bfloat16)
    returned = lax.all_to_all(
        adapter_update.reshape(owners_count, capacity, adapter_update.shape[1]),
        "adapter",
        split_axis=0,
        concat_axis=0,
        tiled=True,
    )
    returned = returned.reshape(owners_count * capacity, adapter_update.shape[1])
    mine = returned[target]
    base = base_product(tokens, value_base_weight)
    return (base + mine.astype(jnp.float32)).astype(jnp.bfloat16)


def solution(mesh):
    return jax.shard_map(
        local,
        mesh=mesh,
        in_specs=(
            P("adapter", "tensor"),
            P("adapter"),
            P(),
            P("tensor", None),
            P("adapter", None, "tensor"),
            P("adapter", None, "tensor"),
        ),
        out_specs=P("adapter", "tensor"),
        check_vma=False,
    )
```

profile of v0, /device:TPU:1, one launch (start us, length us, event | category | flops | bytes accessed | tf_op | source)
XLA Modules:
  0.0 167.9 jit_solution(920119356436640082)
XLA Ops:
  6.5 0.0 copy-start
  6.5 1.6 copy-done
  8.1 3.8 %fusion.19 = f32[512,1024]{1,0:T(8,128)} fusion(bf16[512,1024]{1,0:T(8,128)(2,1)} %param.6, bf16[1024,1024]{1,0:T(8,128)(2,1)S(1)} %copy-done), kind=kOutput, calls=%fused_computation.52 | convolution fusion | flops 1073741824 | bytes 5242880 | tf_op jit(solution)/shard_map/dot_general | solution.py:10
  12.0 0.0 reduce-scatter.2.cloned.1.call-update
  12.0 0.7 copy-done.1
  12.6 0.2 select_reduce_fusion
  12.9 1.2 reduce-window.6
  14.1 0.2 slice_reduce_fusion
  14.4 0.1 fusion.8
  14.6 2.4 %scatter_custom_fusion = s32[640]{0:T(1024)S(1)} fusion(s32[512]{0:T(512)S(1)} %bitcast.52, s32[512]{0:T(512)S(1)} %get-tuple-element.7, s32[]{:T(128)} %constant.34.clone.1), kind=kCustom, calls=%fused_computation.46 | custom fusion | bytes 2564 | tf_op jit(solution)/shard_map/scatter | solution.py:38
  17.0 0.7 all_to_all.12
  17.8 11.6 %all-to-all-start = ((s32[64,1,10]{2,1,0:T(1,128)}), s32[64,1,10]{2,1,0:T(1,128)S(1)}, u32[]{:S(2)}, u32[]{:S(2)}) async-start(s32[64,1,10]{2,1,0:T(1,128)} %bitcast.5), calls=%async_computation.1 | async-start | bytes 65536 | tf_op jit(solution)/shard_map/all_to_all | solution.py:47
  29.4 3.6 %scatter_custom_fusion.1 = bf16[640,1024]{1,0:T(8,128)(2,1)S(1)} fusion(s32[512]{0:T(512)S(1)} %bitcast.53, bf16[512,1024]{1,0:T(8,128)(2,1)} %param.6, bf16[]{:T(256)} %constant.40.clone.1), kind=kCustom, calls=%fused_computation.8 | custom fusion | bytes 1311232 | tf_op jit(solution)/shard_map/scatter | solution.py:37
  33.0 1.6 reshape.157
  34.5 4.1 %all-to-all-done = s32[64,1,10]{2,1,0:T(1,128)S(1)} async-done(((s32[64,1,10]{2,1,0:T(1,128)}), s32[64,1,10]{2,1,0:T(1,128)S(1)}, u32[]{:S(2)}, u32[]{:S(2)}) %all-to-all-start) | async-done | bytes 2592 | tf_op jit(solution)/shard_map/all_to_all | solution.py:47
  38.6 6.4 %all-to-all-start.1 = ((bf16[64,10,1024]{2,1,0:T(8,128)(2,1)}), bf16[64,10,1024]{2,1,0:T(8,128)(2,1)}, u32[]{:S(2)}, u32[]{:S(2)}) async-start(bf16[64,10,1024]{2,1,0:T(8,128)(2,1)} %reshape.157), calls=%async_computation.2 | async-start | bytes 4194304 | tf_op jit(solution)/shard_map/all_to_all | solution.py:40
  45.1 0.5 broadcast.181
  45.6 0.7 reduce.5
  46.3 0.1 eq.67
  46.4 49.8 %all-to-all-done.1 = bf16[64,10,1024]{2,1,0:T(8,128)(2,1)} async-done(((bf16[64,10,1024]{2,1,0:T(8,128)(2,1)}), bf16[64,10,1024]{2,1,0:T(8,128)(2,1)}, u32[]{:S(2)}, u32[]{:S(2)}) %all-to-all-start.1) | async-done | bytes 1310752 | tf_op jit(solution)/shard_map/all_to_all | solution.py:40
  96.2 2.6 %reshape.185 = bf16[640,1024,1]{1,0,2:T(8,128)(2,1)S(1)} reshape(bf16[64,10,1024]{2,1,0:T(8,128)(2,1)} %all-to-all-done.1) | data formatting | bytes 2621440 | tf_op jit(solution)/shard_map/reshape | solution.py:55
  98.8 0.0 copy-start.3
  98.8 2.2 %fusion.2 = f32[640,64]{0,1:T(8,128)} fusion(bf16[640,1024,1]{1,0,2:T(8,128)(2,1)S(1)} %reshape.185, bf16[2,64,1024]{2,1,0:T(8,128)(2,1)} %param.10, f32[640,2]{0,1:T(2,128)S(1)} %get-tuple-element.6), kind=kOutput, calls=%fused_computation.7 | convolution fusion | flops 167895040 | bytes 1741824 | tf_op jit(solution)/shard_map/yn,vln->yvl/dot_general | solution.py:60
  101.0 31.4 %all-reduce.1 = bf16[640,64]{0,1:T(8,128)(2,1)S(1)} all-reduce(f32[640,64]{0,1:T(8,128)} %fusion.2), channel_id=1, replica_groups=mesh['adapter'=64,'tensor'=8] {'tensor'}, use_global_device_ids=true, to_apply=%region_8.9 | all-reduce | flops 40960 | bytes 245760 | tf_op jit(solution)/shard_map/psum | solution.py:64
  132.4 0.2 fusion.1
  132.7 0.8 reshape.159
  133.5 12.5 %all-to-all-start.2 = ((bf16[64,10,128]{2,1,0:T(8,128)(2,1)}), bf16[64,10,128]{2,1,0:T(8,128)(2,1)S(1)}, u32[]{:S(2)}, u32[]{:S(2)}) async-start(bf16[64,10,128]{2,1,0:T(8,128)(2,1)} %reshape.159), calls=%async_computation.3 | async-start | bytes 524288 | tf_op jit(solution)/shard_map/all_to_all | solution.py:74
  146.0 12.0 %all-to-all-done.2 = bf16[64,10,128]{2,1,0:T(8,128)(2,1)S(1)} async-done(((bf16[64,10,128]{2,1,0:T(8,128)(2,1)}), bf16[64,10,128]{2,1,0:T(8,128)(2,1)S(1)}, u32[]{:S(2)}, u32[]{:S(2)}) %all-to-all-start.2) | async-done | bytes 163872 | tf_op jit(solution)/shard_map/all_to_all | solution.py:74
  158.0 0.1 reshape.160
  158.1 1.3 gather_fusion
  159.4 0.0 reduce-scatter.2.cloned.1.call-done
  159.4 1.6 add_convert_fusion
  (13 shorter events, 0.1 us)
Async XLA Ops:
  6.5 1.6 copy-start
  6.5 152.9 %reduce-scatter.2.cloned.1.call-start = ((), (), s32[]{:S(2)}) async-start(), calls=%async_computation.4 | async-start | bytes 2359296 | tf_op jit(solution)/shard_map/reduce_scatter | solution.py:11
  12.0 0.7 copy-start.1
  12.0 0.7 copy-start.2
  17.8 20.8 %all-to-all-start = ((s32[64,1,10]{2,1,0:T(1,128)}), s32[64,1,10]{2,1,0:T(1,128)S(1)}, u32[]{:S(2)}, u32[]{:S(2)}) async-start(s32[64,1,10]{2,1,0:T(1,128)} %bitcast.5), calls=%async_computation.1 | async-start | bytes 65536 | tf_op jit(solution)/shard_map/all_to_all | solution.py:47
  38.6 57.6 %all-to-all-start.1 = ((bf16[64,10,1024]{2,1,0:T(8,128)(2,1)}), bf16[64,10,1024]{2,1,0:T(8,128)(2,1)}, u32[]{:S(2)}, u32[]{:S(2)}) async-start(bf16[64,10,1024]{2,1,0:T(8,128)(2,1)} %reshape.157), calls=%async_computation.2 | async-start | bytes 4194304 | tf_op jit(solution)/shard_map/all_to_all | solution.py:40
  98.8 33.6 %copy-start.3 = (bf16[2,64,128]{2,1,0:T(8,128)(2,1)S(1)}, bf16[2,64,128]{2,1,0:T(8,128)(2,1)}, u32[]{:S(2)}) copy-start(bf16[2,64,128]{2,1,0:T(8,128)(2,1)} %param.11) | copy-start | bytes 98308
  133.5 24.5 %all-to-all-start.2 = ((bf16[64,10,128]{2,1,0:T(8,128)(2,1)}), bf16[64,10,128]{2,1,0:T(8,128)(2,1)S(1)}, u32[]{:S(2)}, u32[]{:S(2)}) async-start(bf16[64,10,128]{2,1,0:T(8,128)(2,1)} %reshape.159), calls=%async_computation.3 | async-start | bytes 524288 | tf_op jit(solution)/shard_map/all_to_all | solution.py:74
Sparse Core Ops, SparseCore 0:
  12.1 46.8 reduce-scatter.1
where the time goes:
time: 169 us; the launch traced here: 168 us
  waiting for transfers between devices  65.9 us (39%)
  blocking collectives  31.4 us (19%)
  starting transfers between devices  30.6 us (18%)
  local copies, waits for them, and re-layouts  16.2 us (10%)
  between operations  13.5 us (8%)
  matrix products  6.25 us (4%)
  other arithmetic  4.02 us (2%)
    all_to_all x1, waiting for transfers between devices, local(): lax.all_to_all(send_rows.reshape(owners_count, capacity, width), 'adapter...  49.8 us
    psum x1, blocking collectives, local(): shrunk = lax.psum(partial_value, 'tensor').astype(jnp.bfloat16)  31.4 us
    all_to_all x1, starting transfers between devices, local(): lax.all_to_all(adapter_update.reshape(owners_count, capacity, adapter_upd...  12.5 us
    all_to_all x1, waiting for transfers between devices, local(): lax.all_to_all(adapter_update.reshape(owners_count, capacity, adapter_upd...  12 us
    all_to_all x1, starting transfers between devices, local(): lax.all_to_all(send_place.reshape(owners_count, capacity), 'adapter', spl...  11.6 us
    all_to_all x1, starting transfers between devices, local(): lax.all_to_all(send_rows.reshape(owners_count, capacity, width), 'adapter...  6.45 us
    all_to_all x1, waiting for transfers between devices, local(): lax.all_to_all(send_place.reshape(owners_count, capacity), 'adapter', spl...  4.07 us
    dot_general x1, matrix products, base_product(): jnp.dot(tokens, value_base_weight, preferred_element_type=jnp.float32)  3.83 us
  transfers between devices with their start and end apart: 4, of which 3 were waited for; matrix products, arithmetic and copies ran while one was open for 11% of the time, Pallas kernels for 0%

commit v1 on v0

v1 whole, which is shorter than its diff:
```python
import jax
import jax.numpy as jnp
from jax import lax
from jax.experimental import pallas as pl
from jax.experimental.pallas import tpu as pltpu
from jax.sharding import PartitionSpec as P

MESH = pl.DeviceIdType.MESH
BF16, F32, I32 = jnp.bfloat16, jnp.float32, jnp.int32

X, Y, CORES, Z = 4, 8, 2, 8
ROWS, WIDTH, OUT = 512, 1024, 128
CAP, RANK = 10, 64
SLOTS = CORES * CAP
BLOCK = Y * SLOTS
ALL = X * BLOCK
SUBS = 4
HELD = 2 * RANK
SUB = HELD // SUBS
HALF = ROWS // 2
PIECE = BLOCK // 4
PADDED = 48
OFFSETS = (0, 1, 7, 2, 6, 3, 5, 4)
adapter_scale = 2.0


def dot(a, b):
    return jnp.dot(a, b, preferred_element_type=F32)


def dot_nt(a, b):
    return lax.dot_general(a, b, (((1,), (1,)), ((), ())), preferred_element_type=F32)


def dot_tn(a, b):
    return lax.dot_general(a, b, (((0,), (0,)), ((), ())), preferred_element_type=F32)


def iota(shape, axis):
    return lax.broadcasted_iota(I32, shape, axis)


def kernel(
    idx_ref,
    stored_ref,
    tok_hbm,
    w_hbm,
    down_hbm,
    up_hbm,
    out_ref,
    tok,
    w,
    down,
    up,
    perm,
    send_rows,
    rows,
    send_place,
    place,
    part,
    ring_out,
    ring_in,
    acc,
    packed,
    sums,
    shrunk,
    back_out,
    back,
    sel,
    delta,
    local_sem,
    y_send,
    y_recv,
    core_send,
    core_recv,
    up_send,
    up_recv,
    x_send,
    x_recv,
    ring_send,
    ring_recv,
    sum_send,
    sum_recv,
    all_send,
    all_recv,
    back_send,
    back_recv,
):
    a = lax.axis_index("adapter")
    z = lax.axis_index("tensor")
    x, y, c = a // (Y * CORES), (a // CORES) % Y, a % CORES

    def device(dx=0, dy=0, dc=0, dz=0):
        ax = lax.rem(x + (dx + X), X)
        ay = lax.rem(y + (dy + Y), Y)
        ac = lax.rem(c + dc, CORES)
        return ((ax * Y + ay) * CORES + ac, lax.rem(z + (dz + Z), Z))

    def remote(src, dst, send, recv, **to):
        return pltpu.make_async_remote_copy(
            src_ref=src,
            dst_ref=dst,
            send_sem=send,
            recv_sem=recv,
            device_id=device(**to),
            device_id_type=MESH,
        )

    started = []

    def go(copy):
        copy.start()
        started.append(copy)

    barrier = pltpu.get_barrier_semaphore()
    partners = [dict(dc=1)]
    partners += [dict(dx=d) for d in range(1, X)]
    partners += [dict(dy=d) for d in range(1, Y)]
    partners += [dict(dz=d) for d in range(1, Z)]
    for to in partners:
        pl.semaphore_signal(barrier, inc=1, device_id=device(**to), device_id_type=MESH)
    load_down = pltpu.make_async_copy(down_hbm, down.at[0, c], local_sem.at[0])
    load_tok = pltpu.make_async_copy(tok_hbm, tok, local_sem.at[1])
    load_w = pltpu.make_async_copy(w_hbm, w, local_sem.at[2])
    load_up = pltpu.make_async_copy(up_hbm, up.at[c, 0], local_sem.at[3])
    for load in (load_down, load_tok, load_w, load_up):
        load.start()

    def y_slot(way, hop):
        return (Y - hop) % Y if way == 0 else hop

    def y_copy(way, hop, sub):
        span = pl.ds(sub * SUB, SUB)
        return remote(
            down.at[y_slot(way, hop - 1), c, span],
            down.at[y_slot(way, hop), c, span],
            y_send.at[way, hop - 1, sub],
            y_recv.at[way, hop - 1, sub],
            dy=1 if way == 0 else -1,
        )

    def y_subs(way, hop):
        order = (0, 1, 2, 3) if way == 0 else (2, 3, 0, 1)
        return order[:2] if hop == Y // 2 else order

    def core_copy(slot):
        return remote(
            down.at[slot, c], down.at[slot, c], core_send.at[slot], core_recv.at[slot], dc=1
        )

    def core_arrival(slot):
        return remote(
            down.at[slot, 1 - c], down.at[slot, 1 - c], core_send.at[slot], core_recv.at[slot], dc=1
        )

    idx = idx_ref[...]
    stored = jnp.broadcast_to(stored_ref[...].astype(F32), (8, 128)).astype(BF16)
    lookup = jnp.where(iota((128, ROWS), 0) == idx, 1.0, 0.0).astype(BF16)
    slot = dot(stored, lookup)[0:1].astype(I32)
    owner = slot // 2
    within = slot - owner * 2
    member = jnp.where(iota((64, ROWS), 0) == owner, 1.0, 0.0)
    earlier = jnp.where(iota((ROWS, ROWS), 0) < iota((ROWS, ROWS), 1), 1.0, 0.0).astype(BF16)
    before = jnp.sum(dot(member.astype(BF16), earlier) * member, axis=0, keepdims=True)
    owner_x, owner_y, owner_c = owner // 16, (owner // 2) & 7, owner & 1
    step_x = (owner_x - x) & 3
    step_y = (owner_y - y) & 7
    position = jnp.where(
        step_y == 0, 0, jnp.where(step_y <= 4, 2 * step_y - 1, 2 * (8 - step_y))
    )
    target = step_x * BLOCK + position * SLOTS + owner_c * CAP + before.astype(I32)
    perm[...] = jnp.where(iota((ALL + 128, ROWS), 0) == target, 1.0, 0.0).astype(BF16)
    within16 = jnp.broadcast_to(within.astype(F32), (16, ROWS)).astype(BF16)

    load_down.wait()
    load_up.wait()
    pl.semaphore_wait(barrier, len(partners))
    for i in range(SUBS):
        for way in range(2):
            go(y_copy(way, 1, y_subs(way, 1)[i]))
    go(core_copy(0))

    def x_copies(dx):
        return (
            remote(
                send_rows.at[dx - 1], rows.at[dx], x_send.at[0, dx - 1], x_recv.at[0, dx - 1], dx=dx
            ),
            remote(
                send_place.at[dx - 1],
                place.at[dx],
                x_send.at[1, dx - 1],
                x_recv.at[1, dx - 1],
                dx=dx,
            ),
        )

    load_tok.wait()
    for dx in (2, 1, 3, 0):
        block = dot(perm[dx * BLOCK : (dx + 1) * BLOCK, :], tok[...]).astype(BF16)
        where = dot_nt(within16, perm[dx * BLOCK : dx * BLOCK + 256, :]).astype(BF16)
        if dx:
            send_rows[dx - 1] = block
            send_place[dx - 1] = where
            for copy in x_copies(dx):
                go(copy)
        else:
            rows[0] = block
            place[0] = where

    def product(m):
        k = lax.rem(z + m, Z)
        part[m] = dot(tok[...], w[:, pl.ds(pl.multiple_of(k * OUT, OUT), OUT)])

    def ring_copy(way, step, half):
        return remote(
            ring_out.at[way, step - 1, half],
            ring_in.at[way, step - 1, half],
            ring_send.at[way, step - 1, half],
            ring_recv.at[way, step - 1, half],
            dz=1 if way == 0 else -1,
        )

    def ring_m(way, step):
        return 5 - step if way == 0 else 3 + step

    def ring_pass(way, step, half, arrived):
        m = ring_m(way, step)
        value = part[m, half * HALF : (half + 1) * HALF, :]
        if arrived:
            ring_copy(way, step - 1, half).wait_recv()
            value = value + ring_in[way, step - 2, half].astype(F32)
        ring_out[way, step - 1, half] = value.astype(BF16)
        go(ring_copy(way, step, half))

    load_w.wait()
    product(4)
    for way in range(2):
        ring_pass(way, 1, way, False)
    product(3)
    ring_pass(0, 2, 1, False)
    product(5)
    ring_pass(1, 2, 0, False)

    def y_forward(hop, i):
        for way in range(2):
            sub = y_subs(way, hop)[i]
            y_copy(way, hop, sub).wait_recv()
            if hop < Y // 2 and sub in y_subs(way, hop + 1):
                go(y_copy(way, hop + 1, sub))

    def ring_step(step):
        for way in range(2):
            first = way
            halves = (first,) if step == 1 else (first, 1 - first)
            for half in halves:
                ring_pass(way, step + 1, half, True)

    fillers = {(1, 0): (2, 6), (1, 1): (1, 7), (1, 2): (0,)}
    for hop in range(1, 4):
        for i in range(SUBS):
            y_forward(hop, i)
            for m in fillers.get((hop, i), ()):
                product(m)
            if i == 2:
                ring_step(hop)
        go(core_copy(y_slot(0, hop)))
        go(core_copy(y_slot(1, hop)))

    def up_copy(dy):
        return remote(
            up.at[c, 0], up.at[c, Y - dy], up_send.at[dy - 1], up_recv.at[dy - 1], dy=dy
        )

    for dy in (4, 3, 5, 2, 6, 1, 7):
        go(up_copy(dy))

    acc[...] = jnp.zeros(acc.shape, F32)
    eye = iota((BLOCK, 256), 0) == iota((BLOCK, 256), 1)
    ones = jnp.ones((256, 128), BF16)
    for dx in (0, 1, 3, 2):
        if dx:
            for copy in x_copies(dx):
                copy.wait_recv()
        spread = jnp.where(eye, place[dx, 0:1, :].astype(F32), 0.0).astype(BF16)
        sel[dx] = jnp.where(
            dot(spread, ones).astype(I32) == iota((BLOCK, 128), 1) // RANK, 1.0, 0.0
        )

    def window(p):
        return (p * SLOTS) // 16 * 16

    def core_masks(p):
        row = window(p) + iota((X, 32, 128), 1) - p * SLOTS
        return [
            jnp.where((row >= k * CAP) & (row < (k + 1) * CAP), 1.0, 0.0) for k in range(CORES)
        ]

    def down_project(p):
        slot = OFFSETS[p]
        core_arrival(slot).wait_recv()
        lo = window(p)
        mine = rows[:, lo : lo + 32, :].reshape(X * 32, WIDTH)
        got = dot_nt(mine, down[slot].reshape(CORES * HELD, WIDTH)).reshape(X, 32, 256)
        first, second = core_masks(p)
        kept = got[:, :, :128] * first + got[:, :, 128:] * second
        acc[:, lo : lo + 32, :] += kept * sel[:, lo : lo + 32, :]

    for p in range(7):
        down_project(p)
    for i in range(2):
        y_forward(4, i)
    go(core_copy(4))
    for way in range(2):
        for half in range(2):
            ring_copy(way, 4, half).wait_recv()
            span = slice(half * HALF, (half + 1) * HALF)
            part[0, span, :] += ring_in[way, 3, half].astype(F32)
    down_project(7)

    both = acc[...]
    both = both + jnp.concatenate([both[:, :, RANK:], both[:, :, :RANK]], axis=2)
    low = iota((BLOCK, 128), 1) < RANK
    for pair in range(2):
        side = jnp.where(low, both[2 * pair], both[2 * pair + 1])
        packed[4 * pair : 4 * pair + 4] = side.reshape(4, PIECE, 128)

    def sum_copy(dz):
        return remote(
            packed.at[lax.rem(z + dz, Z)],
            sums.at[dz - 1],
            sum_send.at[dz - 1],
            sum_recv.at[dz - 1],
            dz=dz,
        )

    far_first = (4, 3, 5, 2, 6, 1, 7)
    for dz in far_first:
        go(sum_copy(dz))
    for dy in (1, 7, 2, 6, 3, 5, 4):
        up_copy(dy).wait_recv()
    up_swap = remote(up.at[c], up.at[c], up_send.at[7], up_recv.at[7], dc=1)
    go(up_swap)
    total = packed[z]
    for dz in (1, 7, 2, 6, 3, 5, 4):
        sum_copy(dz).wait_recv()
        total = total + sums[dz - 1]
    shrunk[z] = jnp.concatenate([total, jnp.zeros((PADDED - PIECE, 128), F32)], axis=0).astype(BF16)

    def all_copy(dz):
        return remote(
            shrunk.at[z], shrunk.at[z], all_send.at[dz - 1], all_recv.at[dz - 1], dz=dz
        )

    def all_arrival(dz):
        k = lax.rem(z + (Z - dz), Z)
        return remote(
            shrunk.at[k], shrunk.at[k], all_send.at[dz - 1], all_recv.at[dz - 1], dz=dz
        )

    for dz in far_first:
        go(all_copy(dz))
    remote(up.at[1 - c], up.at[1 - c], up_send.at[7], up_recv.at[7], dc=1).wait_recv()
    for dz in (1, 7, 2, 6, 3, 5, 4):
        all_arrival(dz).wait_recv()

    for pair in range(2):
        whole = shrunk[4 * pair : 4 * pair + 4].astype(F32)[:, :PIECE, :].reshape(BLOCK, 128)
        swapped = jnp.concatenate([whole[:, RANK:], whole[:, :RANK]], axis=1)
        acc[2 * pair] = jnp.where(low, whole, swapped) * sel[2 * pair]
        acc[2 * pair + 1] = jnp.where(low, swapped, whole) * sel[2 * pair + 1]
    delta[...] = jnp.zeros(delta.shape, F32)
    for p in range(8):
        lo = window(p)
        mine = acc[:, lo : lo + 32, :]
        first, second = core_masks(p)
        wide = jnp.concatenate([mine * first, mine * second], axis=2).astype(BF16)
        maps = up[:, OFFSETS[p]].reshape(CORES * HELD, OUT)
        got = dot(wide.reshape(X * 32, 256), maps).reshape(X, 32, OUT)
        delta[:, lo : lo + 32, :] += got

    def back_copy(dx):
        return remote(
            back_out.at[dx - 1], back.at[dx], back_send.at[dx - 1], back_recv.at[dx - 1], dx=-dx
        )

    for dx in (2, 1, 3, 0):
        block = delta[dx]
        block = (adapter_scale * block).astype(BF16)
        if dx:
            back_out[dx - 1] = block
            go(back_copy(dx))
        else:
            back[0] = block
    for dx in (1, 3, 2):
        back_copy(dx).wait_recv()
    mine = dot_tn(perm[0:ALL, :], back[...].reshape(ALL, OUT))
    out_ref[...] = (part[0] + mine).astype(BF16)

    for copy in started:
        copy.wait_send()


def local(
    tokens,
    token_adapter_index,
    adapter_stored_row,
    value_base_weight,
    adapter_down_maps,
    adapter_up_maps,
):
    vmem = pl.BlockSpec(memory_space=pltpu.VMEM)
    hbm = pl.BlockSpec(memory_space=pl.ANY)
    dma = pltpu.SemaphoreType.DMA
    return pl.pallas_call(
        kernel,
        out_shape=jax.ShapeDtypeStruct((ROWS, OUT), BF16),
        in_specs=[vmem, vmem, hbm, hbm, hbm, hbm],
        out_specs=vmem,
        scratch_shapes=[
            pltpu.VMEM((ROWS, WIDTH), BF16),
            pltpu.VMEM((WIDTH, Z * OUT), BF16),
            pltpu.VMEM((Y, CORES, HELD, WIDTH), BF16),
            pltpu.VMEM((CORES, Y, HELD, OUT), BF16),
            pltpu.VMEM((ALL + 128, ROWS), BF16),
            pltpu.VMEM((X - 1, BLOCK, WIDTH), BF16),
            pltpu.VMEM((X, BLOCK, WIDTH), BF16),
            pltpu.VMEM((X - 1, 16, 256), BF16),
            pltpu.VMEM((X, 16, 256), BF16),
            pltpu.VMEM((Z, ROWS, OUT), F32),
            pltpu.VMEM((2, 4, 2, HALF, OUT), BF16),
            pltpu.VMEM((2, 4, 2, HALF, OUT), BF16),
            pltpu.VMEM((X, BLOCK, 128), F32),
            pltpu.VMEM((Z, PIECE, 128), F32),
            pltpu.VMEM((Z - 1, PIECE, 128), F32),
            pltpu.VMEM((Z, PADDED, 128), BF16),
            pltpu.VMEM((X - 1, BLOCK, OUT), BF16),
            pltpu.VMEM((X, BLOCK, OUT), BF16),
            pltpu.VMEM((X, BLOCK, 128), F32),
            pltpu.VMEM((X, BLOCK, OUT), F32),
            dma((4,)),
            dma((2, 4, SUBS)),
            dma((2, 4, SUBS)),
            dma((Y,)),
            dma((Y,)),
            dma((Y,)),
            dma((Y,)),
            dma((2, X - 1)),
            dma((2, X - 1)),
            dma((2, 4, 2)),
            dma((2, 4, 2)),
            dma((Z - 1,)),
            dma((Z - 1,)),
            dma((Z - 1,)),
            dma((Z - 1,)),
            dma((X - 1,)),
            dma((X - 1,)),
        ],
        compiler_params=pltpu.CompilerParams(
            collective_id=0, has_side_effects=True, vmem_limit_bytes=60 << 20
        ),
        cost_estimate=pl.CostEstimate(
            flops=5_000_000_000, bytes_accessed=3_700_000, transcendentals=0
        ),
    )(
        token_adapter_index.reshape(1, ROWS),
        adapter_stored_row.reshape(1, -1),
        tokens,
        value_base_weight,
        adapter_down_maps.reshape(HELD, WIDTH),
        adapter_up_maps.reshape(HELD, OUT),
    )


def solution(mesh):
    return jax.shard_map(
        local,
        mesh=mesh,
        in_specs=(
            P("adapter", "tensor"),
            P("adapter"),
            P(),
            P("tensor", None),
            P("adapter", None, "tensor"),
            P("adapter", None, "tensor"),
        ),
        out_specs=P("adapter", "tensor"),
        check_vma=False,
    )
```

time: 169 us -> 59.6 us (0.35)
  waiting for transfers between devices: 65.9 us -> 0 us
  Pallas kernels: 0 us -> 57.9 us
  blocking collectives: 31.4 us -> 0 us
  starting transfers between devices: 30.6 us -> 0 us
  local copies, waits for them, and re-layouts: 16.2 us -> 1.57 us
  between operations: 13.5 us -> 0.01 us
  matrix products: 6.25 us -> 0 us
  other arithmetic: 4.02 us -> 0 us
    all_to_all x3 -> x0, waiting for transfers between devices: 65.8 us -> none  [the longest x1 49.8 us: local(): lax.all_to_all(send_rows.reshape(owners_count, capacity, width), 'adapter...]
    pallas_call x0 -> x1, Pallas kernels: none -> 57.9 us  [local(): pl.pallas_call(kernel, out_shape=jax.ShapeDtypeStruct((ROWS, OUT), BF16),...]
    psum x1 -> x0, blocking collectives: 31.4 us -> none  [local(): shrunk = lax.psum(partial_value, 'tensor').astype(jnp.bfloat16)]
    all_to_all x3 -> x0, starting transfers between devices: 30.6 us -> none  [the longest x1 12.5 us: local(): lax.all_to_all(adapter_update.reshape(owners_count, capacity, adapter_upd...]
    dot_general x3 -> x0, matrix products: 6.25 us -> none  [the longest x1 3.83 us: base_product(): jnp.dot(tokens, value_base_weight, preferred_element_type=jnp.float32)]
    scatter x2 -> x0, local copies, waits for them, and re-layouts: 6.02 us -> none  [the longest x1 3.58 us: local(): jnp.zeros((owners_count * capacity, width), jnp.bfloat16).at[target]]
    reshape x4 -> x0, local copies, waits for them, and re-layouts: 4.97 us -> none  [the longest x1 2.57 us: local(): received_rows = received_rows.reshape(owners_count * capacity, width)]
  transfers between devices with their start and end apart: 4 -> 0, of which waited for: 3 -> 0; matrix products, arithmetic and copies ran while one was open for 11% -> 0% of each run, Pallas kernels for 0% -> 0%
where the time goes in v1:
time: 59.6 us; the launch traced here: 59.5 us
  Pallas kernels  57.9 us (97%)
  local copies, waits for them, and re-layouts  1.57 us (3%)
    pallas_call x1, Pallas kernels, local(): pl.pallas_call(kernel, out_shape=jax.ShapeDtypeStruct((ROWS, OUT), BF16),...  57.9 us
    unnamed x1, local copies, waits for them, and re-layouts  1.57 us

profile of v1, /device:TPU:1, one launch (start us, length us, event | category | flops | bytes accessed | tf_op | source)
XLA Modules:
  0.0 59.5 jit_solution(13414097927997049582)
XLA Ops:
  0.0 57.9 %shard_map.64 = bf16[512,128]{1,0:T(8,128)(2,1)} custom-call(s32[1,512]{1,0:T(1,128)} %bitcast.6, s32[1,128]{1,0:T(1,128)} %bitcast.7, bf16[512,1024]{1,0:T(8,128)(2,1)} %tok_hbm.1, bf16[1024,1024]{1,0:T(8,128)(2,1)} %w_hbm.1, bf16[128,1024]{1,0:T(8,128)(2,1)} %bitcast.4, bf16[128,128]{1,0:T(8,128)(2,1)} %bitcast.5), custom_call_target="tpu_custom_call" | custom-call | flops 5000000000 | bytes 3700000 | tf_op jit(solution)/shard_map/pallas_call | solution.py:414
  57.9 1.6 %copy.8 = bf16[512,128]{1,0:T(8,128)(2,1)} copy(bf16[512,128]{1,0:T(8,128)(2,1)} %shard_map.64) | data formatting | bytes 262144

commit v2 on v1

--- a/solution.py
+++ b/solution.py
@@ -11,6 +11,8 @@
 X, Y, CORES, Z = 4, 8, 2, 8
 ROWS, WIDTH, OUT = 512, 1024, 128
 CAP, RANK = 10, 64
+FAR = Y // 2
+LATE = 24
 SLOTS = CORES * CAP
 BLOCK = Y * SLOTS
 ALL = X * BLOCK
@@ -32,27 +34,26 @@
     return lax.dot_general(a, b, (((1,), (1,)), ((), ())), preferred_element_type=F32)
 
 
-def dot_tn(a, b):
-    return lax.dot_general(a, b, (((0,), (0,)), ((), ())), preferred_element_type=F32)
-
-
 def iota(shape, axis):
     return lax.broadcasted_iota(I32, shape, axis)
 
 
 def kernel(
-    idx_ref,
-    stored_ref,
+    idx_hbm,
+    stored_hbm,
     tok_hbm,
     w_hbm,
     down_hbm,
     up_hbm,
     out_ref,
+    idx_ref,
+    stored_ref,
     tok,
     w,
     down,
     up,
     perm,
+    perm_t,
     send_rows,
     rows,
     send_place,
@@ -64,6 +65,8 @@
     packed,
     sums,
     shrunk,
+    late_out,
+    late_in,
     back_out,
     back,
     sel,
@@ -83,6 +86,8 @@
     sum_recv,
     all_send,
     all_recv,
+    late_send,
+    late_recv,
     back_send,
     back_recv,
 ):
@@ -106,7 +111,7 @@
             device_id_type=MESH,
         )
 
-    started = []
+    started, slow = [], []
 
     def go(copy):
         copy.start()
@@ -119,11 +124,13 @@
     partners += [dict(dz=d) for d in range(1, Z)]
     for to in partners:
         pl.semaphore_signal(barrier, inc=1, device_id=device(**to), device_id_type=MESH)
+    load_idx = pltpu.make_async_copy(idx_hbm, idx_ref, local_sem.at[4])
+    load_stored = pltpu.make_async_copy(stored_hbm, stored_ref, local_sem.at[5])
     load_down = pltpu.make_async_copy(down_hbm, down.at[0, c], local_sem.at[0])
     load_tok = pltpu.make_async_copy(tok_hbm, tok, local_sem.at[1])
     load_w = pltpu.make_async_copy(w_hbm, w, local_sem.at[2])
     load_up = pltpu.make_async_copy(up_hbm, up.at[c, 0], local_sem.at[3])
-    for load in (load_down, load_tok, load_w, load_up):
+    for load in (load_down, load_idx, load_stored, load_tok, load_up, load_w):
         load.start()
 
     def y_slot(way, hop):
@@ -140,8 +147,9 @@
         )
 
     def y_subs(way, hop):
-        order = (0, 1, 2, 3) if way == 0 else (2, 3, 0, 1)
-        return order[:2] if hop == Y // 2 else order
+        first, last = range(SUBS // 2), range(SUBS // 2, SUBS)
+        order = (*first, *last) if way == 0 else (*last, *first)
+        return order[: SUBS // 2] if hop == Y // 2 else order
 
     def core_copy(slot):
         return remote(
@@ -153,6 +161,24 @@
             down.at[slot, 1 - c], down.at[slot, 1 - c], core_send.at[slot], core_recv.at[slot], dc=1
         )
 
+    load_down.wait()
+    pl.semaphore_wait(barrier, len(partners))
+    for i in range(SUBS):
+        for way in range(2):
+            go(y_copy(way, 1, y_subs(way, 1)[i]))
+
+    def piece_copy(sub, core):
+        span = pl.ds(sub * SUB, SUB)
+        return remote(
+            down.at[FAR, core, span],
+            down.at[FAR, core, span],
+            core_send.at[Y + sub],
+            core_recv.at[Y + sub],
+            dc=1,
+        )
+
+    load_idx.wait()
+    load_stored.wait()
     idx = idx_ref[...]
     stored = jnp.broadcast_to(stored_ref[...].astype(F32), (8, 128)).astype(BF16)
     lookup = jnp.where(iota((128, ROWS), 0) == idx, 1.0, 0.0).astype(BF16)
@@ -172,14 +198,6 @@
     perm[...] = jnp.where(iota((ALL + 128, ROWS), 0) == target, 1.0, 0.0).astype(BF16)
     within16 = jnp.broadcast_to(within.astype(F32), (16, ROWS)).astype(BF16)
 
-    load_down.wait()
-    load_up.wait()
-    pl.semaphore_wait(barrier, len(partners))
-    for i in range(SUBS):
-        for way in range(2):
-            go(y_copy(way, 1, y_subs(way, 1)[i]))
-    go(core_copy(0))
-
     def x_copies(dx):
         return (
             remote(
@@ -195,14 +213,15 @@
         )
 
     load_tok.wait()
-    for dx in (2, 1, 3, 0):
+    for dx in (1, 3, 2, 0):
         block = dot(perm[dx * BLOCK : (dx + 1) * BLOCK, :], tok[...]).astype(BF16)
         where = dot_nt(within16, perm[dx * BLOCK : dx * BLOCK + 256, :]).astype(BF16)
         if dx:
             send_rows[dx - 1] = block
             send_place[dx - 1] = where
             for copy in x_copies(dx):
-                go(copy)
+                copy.start()
+                slow.append(copy)
         else:
             rows[0] = block
             place[0] = where
@@ -232,6 +251,8 @@
         ring_out[way, step - 1, half] = value.astype(BF16)
         go(ring_copy(way, step, half))
 
+    go(core_copy(0))
+    load_up.wait()
     load_w.wait()
     product(4)
     for way in range(2):
@@ -245,7 +266,9 @@
         for way in range(2):
             sub = y_subs(way, hop)[i]
             y_copy(way, hop, sub).wait_recv()
-            if hop < Y // 2 and sub in y_subs(way, hop + 1):
+            if hop == FAR:
+                go(piece_copy(sub, c))
+            elif sub in y_subs(way, hop + 1):
                 go(y_copy(way, hop + 1, sub))
 
     def ring_step(step):
@@ -255,24 +278,32 @@
             for half in halves:
                 ring_pass(way, step + 1, half, True)
 
-    fillers = {(1, 0): (2, 6), (1, 1): (1, 7), (1, 2): (0,)}
+    def settle():
+        while started:
+            started.pop(0).wait_send()
+
+    fillers = {(1, 0): (2, 6), (1, 1): (1, 7, 0)}
     for hop in range(1, 4):
         for i in range(SUBS):
             y_forward(hop, i)
             for m in fillers.get((hop, i), ()):
                 product(m)
-            if i == 2:
+            if i == SUBS // 2:
                 ring_step(hop)
+        recent = started[-10:]
+        del started[-10:]
+        settle()
+        started.extend(recent)
         go(core_copy(y_slot(0, hop)))
         go(core_copy(y_slot(1, hop)))
+        if hop == 1:
+            perm_t[...] = jnp.transpose(perm[0:ALL, :])
 
     def up_copy(dy):
         return remote(
             up.at[c, 0], up.at[c, Y - dy], up_send.at[dy - 1], up_recv.at[dy - 1], dy=dy
         )
 
-    for dy in (4, 3, 5, 2, 6, 1, 7):
-        go(up_copy(dy))
 
     acc[...] = jnp.zeros(acc.shape, F32)
     eye = iota((BLOCK, 256), 0) == iota((BLOCK, 256), 1)
@@ -297,74 +328,99 @@
 
     def down_project(p):
         slot = OFFSETS[p]
-        core_arrival(slot).wait_recv()
+        if slot == FAR:
+            for sub in range(SUBS):
+                piece_copy(sub, 1 - c).wait_recv()
+        else:
+            core_arrival(slot).wait_recv()
         lo = window(p)
         mine = rows[:, lo : lo + 32, :].reshape(X * 32, WIDTH)
         got = dot_nt(mine, down[slot].reshape(CORES * HELD, WIDTH)).reshape(X, 32, 256)
         first, second = core_masks(p)
         kept = got[:, :, :128] * first + got[:, :, 128:] * second
-        acc[:, lo : lo + 32, :] += kept * sel[:, lo : lo + 32, :]
+        return kept * sel[:, lo : lo + 32, :]
 
     for p in range(7):
-        down_project(p)
-    for i in range(2):
-        y_forward(4, i)
-    go(core_copy(4))
+        lo = window(p)
+        acc[:, lo : lo + 32, :] += down_project(p)
+
+    def side_by_side(found):
+        whole = found + jnp.concatenate([found[:, :, RANK:], found[:, :, :RANK]], axis=2)
+        low = iota(whole.shape[1:], 1) < RANK
+        return [jnp.where(low, whole[2 * pair], whole[2 * pair + 1]) for pair in range(2)]
+
+    for pair, side in enumerate(side_by_side(acc[...])):
+        packed[4 * pair : 4 * pair + 4] = side.reshape(4, PIECE, 128)
+
+    def sum_copy(dz):
+        return remote(
+            packed.at[lax.rem(z + dz, Z)],
+            sums.at[dz - 1],
+            sum_send.at[dz - 1],
+            sum_recv.at[dz - 1],
+            dz=dz,
+        )
+
+    far_first = (4, 3, 5, 2, 6, 1, 7)
+    for dz in far_first:
+        go(sum_copy(dz))
+    def late_copy(dz):
+        return remote(
+            late_out, late_in.at[dz - 1], late_send.at[dz - 1], late_recv.at[dz - 1], dz=dz
+        )
+
+    for i in range(SUBS // 2):
+        y_forward(FAR, i)
+    for dy in far_first:
+        go(up_copy(dy))
+    for pair, side in enumerate(side_by_side(down_project(7)[:, 32 - LATE :, :])):
+        late_out[pair * LATE : (pair + 1) * LATE, :] = side.astype(BF16)
+    for dz in far_first:
+        go(late_copy(dz))
+
+    total = packed[z]
+    for dz in (1, 7, 2, 6, 3, 5, 4):
+        sum_copy(dz).wait_recv()
+        total = total + sums[dz - 1]
+    shrunk[z] = jnp.concatenate([total, jnp.zeros((PADDED - PIECE, 128), F32)], axis=0).astype(BF16)
+
+    def all_copy(dz):
+        return remote(
+            shrunk.at[z], shrunk.at[z], all_send.at[dz - 1], all_recv.at[dz - 1], dz=dz
+        )
+
+    def all_arrival(dz):
+        k = lax.rem(z + (Z - dz), Z)
+        return remote(
+            shrunk.at[k], shrunk.at[k], all_send.at[dz - 1], all_recv.at[dz - 1], dz=dz
+        )
+
+    for dz in far_first:
+        go(all_copy(dz))
     for way in range(2):
         for half in range(2):
             ring_copy(way, 4, half).wait_recv()
             span = slice(half * HALF, (half + 1) * HALF)
             part[0, span, :] += ring_in[way, 3, half].astype(F32)
-    down_project(7)
-
-    both = acc[...]
-    both = both + jnp.concatenate([both[:, :, RANK:], both[:, :, :RANK]], axis=2)
+    late = late_out[...].astype(F32)
+    for dz in (1, 7, 2, 6, 3, 5, 4):
+        late_copy(dz).wait_recv()
+        late = late + late_in[dz - 1].astype(F32)
+    late = late.astype(BF16).astype(F32)
+    for dy in (1, 7, 2, 6, 3, 5, 4):
+        up_copy(dy).wait_recv()
+    go(remote(up.at[c], up.at[c], up_send.at[7], up_recv.at[7], dc=1))
+    for dz in (1, 7, 2, 6, 3, 5, 4):
+        all_arrival(dz).wait_recv()
+    remote(up.at[1 - c], up.at[1 - c], up_send.at[7], up_recv.at[7], dc=1).wait_recv()
+
     low = iota((BLOCK, 128), 1) < RANK
     for pair in range(2):
-        side = jnp.where(low, both[2 * pair], both[2 * pair + 1])
-        packed[4 * pair : 4 * pair + 4] = side.reshape(4, PIECE, 128)
-
-    def sum_copy(dz):
-        return remote(
-            packed.at[lax.rem(z + dz, Z)],
-            sums.at[dz - 1],
-            sum_send.at[dz - 1],
-            sum_recv.at[dz - 1],
-            dz=dz,
-        )
-
-    far_first = (4, 3, 5, 2, 6, 1, 7)
-    for dz in far_first:
-        go(sum_copy(dz))
-    for dy in (1, 7, 2, 6, 3, 5, 4):
-        up_copy(dy).wait_recv()
-    up_swap = remote(up.at[c], up.at[c], up_send.at[7], up_recv.at[7], dc=1)
-    go(up_swap)
-    total = packed[z]
-    for dz in (1, 7, 2, 6, 3, 5, 4):
-        sum_copy(dz).wait_recv()
-        total = total + sums[dz - 1]
-    shrunk[z] = jnp.concatenate([total, jnp.zeros((PADDED - PIECE, 128), F32)], axis=0).astype(BF16)
-
-    def all_copy(dz):
-        return remote(
-            shrunk.at[z], shrunk.at[z], all_send.at[dz - 1], all_recv.at[dz - 1], dz=dz
-        )
-
-    def all_arrival(dz):
-        k = lax.rem(z + (Z - dz), Z)
-        return remote(
-            shrunk.at[k], shrunk.at[k], all_send.at[dz - 1], all_recv.at[dz - 1], dz=dz
-        )
-
-    for dz in far_first:
-        go(all_copy(dz))
-    remote(up.at[1 - c], up.at[1 - c], up_send.at[7], up_recv.at[7], dc=1).wait_recv()
-    for dz in (1, 7, 2, 6, 3, 5, 4):
-        all_arrival(dz).wait_recv()
-
-    for pair in range(2):
         whole = shrunk[4 * pair : 4 * pair + 4].astype(F32)[:, :PIECE, :].reshape(BLOCK, 128)
+        nearer = jnp.zeros((BLOCK - LATE, 128), F32)
+        whole = whole + jnp.concatenate(
+            [nearer, late[pair * LATE : (pair + 1) * LATE, :]], axis=0
+        )
         swapped = jnp.concatenate([whole[:, RANK:], whole[:, :RANK]], axis=1)
         acc[2 * pair] = jnp.where(low, whole, swapped) * sel[2 * pair]
         acc[2 * pair + 1] = jnp.where(low, swapped, whole) * sel[2 * pair + 1]
@@ -388,16 +444,18 @@
         block = (adapter_scale * block).astype(BF16)
         if dx:
             back_out[dx - 1] = block
-            go(back_copy(dx))
+            back_copy(dx).start()
         else:
             back[0] = block
+    started.extend(slow)
+    settle()
     for dx in (1, 3, 2):
         back_copy(dx).wait_recv()
-    mine = dot_tn(perm[0:ALL, :], back[...].reshape(ALL, OUT))
+    mine = dot(perm_t[...], back[...].reshape(ALL, OUT))
     out_ref[...] = (part[0] + mine).astype(BF16)
 
-    for copy in started:
-        copy.wait_send()
+    for dx in range(1, X):
+        back_copy(dx).wait_send()
 
 
 def local(
@@ -409,19 +467,22 @@
     adapter_up_maps,
 ):
     vmem = pl.BlockSpec(memory_space=pltpu.VMEM)
-    hbm = pl.BlockSpec(memory_space=pl.ANY)
+    hbm = pl.BlockSpec(memory_space=pltpu.HBM)
     dma = pltpu.SemaphoreType.DMA
     return pl.pallas_call(
         kernel,
         out_shape=jax.ShapeDtypeStruct((ROWS, OUT), BF16),
-        in_specs=[vmem, vmem, hbm, hbm, hbm, hbm],
+        in_specs=[hbm] * 6,
         out_specs=vmem,
         scratch_shapes=[
+            pltpu.VMEM((1, ROWS), I32),
+            pltpu.VMEM((1, 2 * Y * X * CORES), I32),
             pltpu.VMEM((ROWS, WIDTH), BF16),
             pltpu.VMEM((WIDTH, Z * OUT), BF16),
             pltpu.VMEM((Y, CORES, HELD, WIDTH), BF16),
             pltpu.VMEM((CORES, Y, HELD, OUT), BF16),
             pltpu.VMEM((ALL + 128, ROWS), BF16),
+            pltpu.VMEM((ROWS, ALL), BF16),
             pltpu.VMEM((X - 1, BLOCK, WIDTH), BF16),
             pltpu.VMEM((X, BLOCK, WIDTH), BF16),
             pltpu.VMEM((X - 1, 16, 256), BF16),
@@ -433,21 +494,25 @@
             pltpu.VMEM((Z, PIECE, 128), F32),
             pltpu.VMEM((Z - 1, PIECE, 128), F32),
             pltpu.VMEM((Z, PADDED, 128), BF16),
+            pltpu.VMEM((2 * LATE, 128), BF16),
+            pltpu.VMEM((Z - 1, 2 * LATE, 128), BF16),
             pltpu.VMEM((X - 1, BLOCK, OUT), BF16),
             pltpu.VMEM((X, BLOCK, OUT), BF16),
             pltpu.VMEM((X, BLOCK, 128), F32),
             pltpu.VMEM((X, BLOCK, OUT), F32),
-            dma((4,)),
+            dma((6,)),
             dma((2, 4, SUBS)),
             dma((2, 4, SUBS)),
-            dma((Y,)),
-            dma((Y,)),
+            dma((Y + SUBS,)),
+            dma((Y + SUBS,)),
             dma((Y,)),
             dma((Y,)),
             dma((2, X - 1)),
             dma((2, X - 1)),
             dma((2, 4, 2)),
             dma((2, 4, 2)),
+            dma((Z - 1,)),
+            dma((Z - 1,)),
             dma((Z - 1,)),
             dma((Z - 1,)),
             dma((Z - 1,)),

time: 59.6 us -> 56.9 us (0.955)
  Pallas kernels: 57.9 us -> 54.9 us
    pallas_call x1, Pallas kernels: 57.9 us -> 54.9 us  [local(): pl.pallas_call(kernel, out_shape=jax.ShapeDtypeStruct((ROWS, OUT), BF16),...]
where the time goes in v2:
time: 56.9 us; the launch traced here: 56.5 us
  Pallas kernels  54.9 us (96%)
  local copies, waits for them, and re-layouts  1.57 us (3%)
    pallas_call x1, Pallas kernels, local(): pl.pallas_call(kernel, out_shape=jax.ShapeDtypeStruct((ROWS, OUT), BF16),...  54.9 us
    unnamed x1, local copies, waits for them, and re-layouts  1.57 us

profile of v2, /device:TPU:1, one launch (start us, length us, event | category | flops | bytes accessed | tf_op | source)
XLA Modules:
  0.0 56.5 jit_solution(17713203118248540414)
XLA Ops:
  0.0 54.9 %shard_map.64 = bf16[512,128]{1,0:T(8,128)(2,1)} custom-call(s32[1,512]{1,0:T(1,128)} %bitcast.6, s32[1,128]{1,0:T(1,128)} %bitcast.7, bf16[512,1024]{1,0:T(8,128)(2,1)} %tok_hbm.1, bf16[1024,1024]{1,0:T(8,128)(2,1)} %w_hbm.1, bf16[128,1024]{1,0:T(8,128)(2,1)} %bitcast.4, bf16[128,128]{1,0:T(8,128)(2,1)} %bitcast.5), custom_call_target="tpu_custom_call" | custom-call | flops 5000000000 | bytes 3700000 | tf_op jit(solution)/shard_map/pallas_call | solution.py:472
  54.9 1.6 %copy.8 = bf16[512,128]{1,0:T(8,128)(2,1)} copy(bf16[512,128]{1,0:T(8,128)(2,1)} %shard_map.64) | data formatting | bytes 262144

commit v3 on v2

v3 whole, which is shorter than its diff:
```python
import jax
import jax.numpy as jnp
from jax import lax
from jax.experimental import pallas as pl
from jax.experimental.pallas import tpu as pltpu
from jax.sharding import PartitionSpec as P

MESH = pl.DeviceIdType.MESH
BF16, F32, I32 = jnp.bfloat16, jnp.float32, jnp.int32

X, Y, CORES, Z = 4, 8, 2, 8
ROWS, WIDTH, OUT = 512, 1024, 128
CAP, RANK = 10, 64
FAR = Y // 2
LATE = 16
BLOCKS = X * CORES
BLOCK = Y * CAP
ALL = BLOCKS * BLOCK
SUBS = 4
HELD = 2 * RANK
SUB = HELD // SUBS
HALF = ROWS // 2
PIECE = BLOCK // 2
PADDED = 48
PAIRS = BLOCKS // 2
OFFSETS = (0, 1, 7, 2, 6, 3, 5, 4)
OTHERS = (2, 6, 3, 7, 4, 5, 1)
adapter_scale = 2.0


def dot(a, b):
    return jnp.dot(a, b, preferred_element_type=F32)


def dot_nt(a, b):
    return lax.dot_general(a, b, (((1,), (1,)), ((), ())), preferred_element_type=F32)


def iota(shape, axis):
    return lax.broadcasted_iota(I32, shape, axis)


def kernel(
    idx_hbm,
    stored_hbm,
    tok_hbm,
    w_hbm,
    down_hbm,
    up_hbm,
    out_ref,
    idx_ref,
    stored_ref,
    tok,
    w,
    down,
    up,
    perm,
    perm_t,
    send_rows,
    rows,
    send_place,
    place,
    part,
    ring_out,
    ring_in,
    acc,
    packed,
    sums,
    shrunk,
    late_out,
    late_in,
    back_out,
    back,
    sel,
    delta,
    local_sem,
    y_send,
    y_recv,
    up_send,
    up_recv,
    x_send,
    x_recv,
    ring_send,
    ring_recv,
    sum_send,
    sum_recv,
    all_send,
    all_recv,
    late_send,
    late_recv,
    back_send,
    back_recv,
):
    a = lax.axis_index("adapter")
    z = lax.axis_index("tensor")
    x, y, c = a // (Y * CORES), (a // CORES) % Y, a % CORES

    def device(dx=0, dy=0, dc=0, dz=0):
        ax = lax.rem(x + (dx + X), X)
        ay = lax.rem(y + (dy + Y), Y)
        ac = lax.rem(c + dc, CORES)
        return ((ax * Y + ay) * CORES + ac, lax.rem(z + (dz + Z), Z))

    def remote(src, dst, send, recv, **to):
        return pltpu.make_async_remote_copy(
            src_ref=src,
            dst_ref=dst,
            send_sem=send,
            recv_sem=recv,
            device_id=device(**to),
            device_id_type=MESH,
        )

    started, slow = [], []

    def go(copy):
        copy.start()
        started.append(copy)

    barrier = pltpu.get_barrier_semaphore()
    partners = [dict(dx=b // 2, dc=b % 2) for b in OTHERS]
    partners += [dict(dy=d) for d in range(1, Y)]
    partners += [dict(dz=d) for d in range(1, Z)]
    for to in partners:
        pl.semaphore_signal(barrier, inc=1, device_id=device(**to), device_id_type=MESH)
    load_idx = pltpu.make_async_copy(idx_hbm, idx_ref, local_sem.at[4])
    load_stored = pltpu.make_async_copy(stored_hbm, stored_ref, local_sem.at[5])
    load_down = pltpu.make_async_copy(down_hbm, down.at[0], local_sem.at[0])
    load_tok = pltpu.make_async_copy(tok_hbm, tok, local_sem.at[1])
    load_w = pltpu.make_async_copy(w_hbm, w, local_sem.at[2])
    load_up = pltpu.make_async_copy(up_hbm, up.at[0], local_sem.at[3])
    for load in (load_down, load_idx, load_stored, load_tok, load_up, load_w):
        load.start()

    def y_slot(way, hop):
        return (Y - hop) % Y if way == 0 else hop

    def y_copy(way, hop, sub):
        span = pl.ds(sub * SUB, SUB)
        return remote(
            down.at[y_slot(way, hop - 1), span],
            down.at[y_slot(way, hop), span],
            y_send.at[way, hop - 1, sub],
            y_recv.at[way, hop - 1, sub],
            dy=1 if way == 0 else -1,
        )

    def y_subs(way, hop):
        first, last = range(SUBS // 2), range(SUBS // 2, SUBS)
        order = (*first, *last) if way == 0 else (*last, *first)
        return order[: SUBS // 2] if hop == Y // 2 else order

    load_down.wait()
    pl.semaphore_wait(barrier, len(partners))
    for i in range(SUBS):
        for way in range(2):
            go(y_copy(way, 1, y_subs(way, 1)[i]))

    def piece_copy(slot, sub, core):
        span = pl.ds(sub * SUB, SUB)
        place = Y + PIECEWISE.index(slot) * SUBS + sub
        return remote(
            down.at[slot, core, span],
            down.at[slot, core, span],
            core_send.at[place],
            core_recv.at[place],
            dc=1,
        )

    load_idx.wait()
    load_stored.wait()
    idx = idx_ref[...]
    stored = jnp.broadcast_to(stored_ref[...].astype(F32), (8, 128)).astype(BF16)
    lookup = jnp.where(iota((128, ROWS), 0) == idx, 1.0, 0.0).astype(BF16)
    slot = dot(stored, lookup)[0:1].astype(I32)
    owner = slot // 2
    within = slot - owner * 2
    member = jnp.where(iota((64, ROWS), 0) == owner, 1.0, 0.0)
    earlier = jnp.where(iota((ROWS, ROWS), 0) < iota((ROWS, ROWS), 1), 1.0, 0.0).astype(BF16)
    before = jnp.sum(dot(member.astype(BF16), earlier) * member, axis=0, keepdims=True)
    owner_x, owner_y, owner_c = owner // 16, (owner // 2) & 7, owner & 1
    step_x = (owner_x - x) & 3
    step_y = (owner_y - y) & 7
    position = jnp.where(
        step_y == 0, 0, jnp.where(step_y <= 4, 2 * step_y - 1, 2 * (8 - step_y))
    )
    block_of = step_x * CORES + ((owner_c - c) & 1)
    target = block_of * BLOCK + position * CAP + before.astype(I32)
    perm[...] = jnp.where(iota((ALL + 128, ROWS), 0) == target, 1.0, 0.0).astype(BF16)
    within16 = jnp.broadcast_to(within.astype(F32), (16, ROWS)).astype(BF16)

    def x_copies(b):
        to = dict(dx=b // 2, dc=b % 2)
        return (
            remote(send_rows.at[b - 1], rows.at[b], x_send.at[0, b - 1], x_recv.at[0, b - 1], **to),
            remote(
                send_place.at[b - 1], place.at[b], x_send.at[1, b - 1], x_recv.at[1, b - 1], **to
            ),
        )

    load_tok.wait()
    for b in (*OTHERS, 0):
        block = dot(perm[b * BLOCK : (b + 1) * BLOCK, :], tok[...]).astype(BF16)
        where = dot_nt(within16, perm[b * BLOCK : b * BLOCK + 128, :]).astype(BF16)
        if b:
            send_rows[b - 1] = block
            send_place[b - 1] = where
            for copy in x_copies(b):
                copy.start()
                slow.append(copy)
        else:
            rows[0] = block
            place[0] = where

    def product(m):
        k = lax.rem(z + m, Z)
        part[m] = dot(tok[...], w[:, pl.ds(pl.multiple_of(k * OUT, OUT), OUT)])

    def ring_copy(way, step, half):
        return remote(
            ring_out.at[way, step - 1, half],
            ring_in.at[way, step - 1, half],
            ring_send.at[way, step - 1, half],
            ring_recv.at[way, step - 1, half],
            dz=1 if way == 0 else -1,
        )

    def ring_m(way, step):
        return 5 - step if way == 0 else 3 + step

    def ring_pass(way, step, half, arrived):
        m = ring_m(way, step)
        value = part[m, half * HALF : (half + 1) * HALF, :]
        if arrived:
            ring_copy(way, step - 1, half).wait_recv()
            value = value + ring_in[way, step - 2, half].astype(F32)
        ring_out[way, step - 1, half] = value.astype(BF16)
        go(ring_copy(way, step, half))

    load_up.wait()
    load_w.wait()
    def y_forward(hop, i):
        for way in range(2):
            sub = y_subs(way, hop)[i]
            y_copy(way, hop, sub).wait_recv()
            if hop < FAR and sub in y_subs(way, hop + 1):
                go(y_copy(way, hop + 1, sub))

    def ring_step(step):
        for way in range(2):
            first = way
            halves = (first,) if step == 1 else (first, 1 - first)
            for half in halves:
                ring_pass(way, step + 1, half, True)

    def settle():
        while started:
            started.pop(0).wait_send()

    product(4)
    for way in range(2):
        ring_pass(way, 1, way, False)
    product(3)
    ring_pass(0, 2, 1, False)
    product(5)
    ring_pass(1, 2, 0, False)
    y_forward(1, 0)
    product(2)
    product(6)
    y_forward(1, 1)
    product(1)
    product(7)
    y_forward(1, 2)
    ring_step(1)
    y_forward(1, 3)
    product(0)
    perm_t[...] = jnp.transpose(perm[0:ALL, :])
    y_forward(2, 0)
    y_forward(2, 1)
    ring_step(2)
    y_forward(2, 2)
    y_forward(2, 3)
    y_forward(3, 0)
    ring_step(3)
    y_forward(3, 1)
    y_forward(3, 2)
    y_forward(3, 3)
    recent = started[-10:]
    del started[-10:]
    settle()
    started.extend(recent)

    def up_copy(dy):
        return remote(
            up.at[0], up.at[Y - dy], up_send.at[dy - 1], up_recv.at[dy - 1], dy=dy
        )


    acc[...] = jnp.zeros(acc.shape, F32)
    eye = iota((BLOCK, 128), 0) == iota((BLOCK, 128), 1)
    ones = jnp.ones((128, 128), BF16)
    for b in (0, *OTHERS):
        if b:
            for copy in x_copies(b):
                copy.wait_recv()
        spread = jnp.where(eye, place[b, 0:1, :].astype(F32), 0.0).astype(BF16)
        sel[b] = jnp.where(
            dot(spread, ones).astype(I32) == iota((BLOCK, 128), 1) // RANK, 1.0, 0.0
        )

    def window(p):
        return min((p * CAP) // 16 * 16, BLOCK - 32)

    def kept_rows(p):
        row = window(p) + iota((BLOCKS, 32, 128), 1) - p * CAP
        return jnp.where((row >= 0) & (row < CAP), 1.0, 0.0) * sel[:, window(p) : window(p) + 32, :]

    def down_project(p):
        lo = window(p)
        mine = rows[:, lo : lo + 32, :].reshape(BLOCKS * 32, WIDTH)
        return dot_nt(mine, down[OFFSETS[p]]).reshape(BLOCKS, 32, 128) * kept_rows(p)

    for p in range(7):
        lo = window(p)
        acc[:, lo : lo + 32, :] += down_project(p)

    def side_by_side(found):
        whole = found + jnp.concatenate([found[:, :, RANK:], found[:, :, :RANK]], axis=2)
        low = iota(whole.shape[1:], 1) < RANK
        return [jnp.where(low, whole[2 * pair], whole[2 * pair + 1]) for pair in range(PAIRS)]

    for pair, side in enumerate(side_by_side(acc[...])):
        side = side.reshape(2, PIECE, 128)
        side = jnp.concatenate([side, jnp.zeros((2, PADDED - PIECE, 128), F32)], axis=1)
        packed[2 * pair : 2 * pair + 2] = side.astype(BF16)

    def sum_copy(dz):
        return remote(
            packed.at[lax.rem(z + dz, Z)],
            sums.at[dz - 1],
            sum_send.at[dz - 1],
            sum_recv.at[dz - 1],
            dz=dz,
        )

    far_first = (4, 3, 5, 2, 6, 1, 7)
    for dz in far_first:
        go(sum_copy(dz))
    def late_copy(dz):
        return remote(
            late_out, late_in.at[dz - 1], late_send.at[dz - 1], late_recv.at[dz - 1], dz=dz
        )

    for i in range(SUBS // 2):
        y_forward(FAR, i)
    for dy in far_first:
        go(up_copy(dy))
    for pair, side in enumerate(side_by_side(down_project(7)[:, 32 - LATE :, :])):
        late_out[pair * LATE : (pair + 1) * LATE, :] = side.astype(BF16)
    for dz in far_first:
        go(late_copy(dz))

    total = packed[z].astype(F32)
    for dz in (1, 7, 2, 6, 3, 5, 4):
        sum_copy(dz).wait_recv()
        total = total + sums[dz - 1].astype(F32)
    shrunk[z] = total.astype(BF16)

    def all_copy(dz):
        return remote(
            shrunk.at[z], shrunk.at[z], all_send.at[dz - 1], all_recv.at[dz - 1], dz=dz
        )

    def all_arrival(dz):
        k = lax.rem(z + (Z - dz), Z)
        return remote(
            shrunk.at[k], shrunk.at[k], all_send.at[dz - 1], all_recv.at[dz - 1], dz=dz
        )

    for dz in far_first:
        go(all_copy(dz))
    for way in range(2):
        for half in range(2):
            ring_copy(way, 4, half).wait_recv()
            span = slice(half * HALF, (half + 1) * HALF)
            part[0, span, :] += ring_in[way, 3, half].astype(F32)
    late = late_out[...].astype(F32)
    for dz in (1, 7, 2, 6, 3, 5, 4):
        late_copy(dz).wait_recv()
        late = late + late_in[dz - 1].astype(F32)
    late = late.astype(BF16).astype(F32)
    for dy in (1, 7, 2, 6, 3, 5, 4):
        up_copy(dy).wait_recv()
    for dz in (1, 7, 2, 6, 3, 5, 4):
        all_arrival(dz).wait_recv()

    low = iota((BLOCK, 128), 1) < RANK
    for pair in range(PAIRS):
        whole = shrunk[2 * pair : 2 * pair + 2].astype(F32)[:, :PIECE, :].reshape(BLOCK, 128)
        nearer = jnp.zeros((BLOCK - LATE, 128), F32)
        whole = whole + jnp.concatenate(
            [nearer, late[pair * LATE : (pair + 1) * LATE, :]], axis=0
        )
        swapped = jnp.concatenate([whole[:, RANK:], whole[:, :RANK]], axis=1)
        acc[2 * pair] = jnp.where(low, whole, swapped) * sel[2 * pair]
        acc[2 * pair + 1] = jnp.where(low, swapped, whole) * sel[2 * pair + 1]
    delta[...] = jnp.zeros(delta.shape, F32)
    for p in range(8):
        lo = window(p)
        mine = (acc[:, lo : lo + 32, :] * kept_rows(p)).astype(BF16)
        got = dot(mine.reshape(BLOCKS * 32, 128), up[OFFSETS[p]])
        delta[:, lo : lo + 32, :] += got.reshape(BLOCKS, 32, OUT)

    def back_copy(b):
        return remote(
            back_out.at[b - 1],
            back.at[b],
            back_send.at[b - 1],
            back_recv.at[b - 1],
            dx=-(b // 2),
            dc=b % 2,
        )

    for b in (5, 4, 7, 3, 6, 2, 1, 0):
        block = (adapter_scale * delta[b]).astype(BF16)
        if b:
            back_out[b - 1] = block
            back_copy(b).start()
        else:
            back[0] = block
    started.extend(slow)
    settle()
    for b in OTHERS:
        back_copy(b).wait_recv()
    mine = dot(perm_t[...], back[...].reshape(ALL, OUT))
    out_ref[...] = (part[0] + mine).astype(BF16)

    for b in OTHERS:
        back_copy(b).wait_send()


def local(
    tokens,
    token_adapter_index,
    adapter_stored_row,
    value_base_weight,
    adapter_down_maps,
    adapter_up_maps,
):
    vmem = pl.BlockSpec(memory_space=pltpu.VMEM)
    hbm = pl.BlockSpec(memory_space=pltpu.HBM)
    dma = pltpu.SemaphoreType.DMA
    return pl.pallas_call(
        kernel,
        out_shape=jax.ShapeDtypeStruct((ROWS, OUT), BF16),
        in_specs=[hbm] * 6,
        out_specs=vmem,
        scratch_shapes=[
            pltpu.VMEM((1, ROWS), I32),
            pltpu.VMEM((1, 2 * Y * X * CORES), I32),
            pltpu.VMEM((ROWS, WIDTH), BF16),
            pltpu.VMEM((WIDTH, Z * OUT), BF16),
            pltpu.VMEM((Y, HELD, WIDTH), BF16),
            pltpu.VMEM((Y, HELD, OUT), BF16),
            pltpu.VMEM((ALL + 128, ROWS), BF16),
            pltpu.VMEM((ROWS, ALL), BF16),
            pltpu.VMEM((BLOCKS - 1, BLOCK, WIDTH), BF16),
            pltpu.VMEM((BLOCKS, BLOCK, WIDTH), BF16),
            pltpu.VMEM((BLOCKS - 1, 16, 128), BF16),
            pltpu.VMEM((BLOCKS, 16, 128), BF16),
            pltpu.VMEM((Z, ROWS, OUT), F32),
            pltpu.VMEM((2, 4, 2, HALF, OUT), BF16),
            pltpu.VMEM((2, 4, 2, HALF, OUT), BF16),
            pltpu.VMEM((BLOCKS, BLOCK, 128), F32),
            pltpu.VMEM((Z, PADDED, 128), BF16),
            pltpu.VMEM((Z - 1, PADDED, 128), BF16),
            pltpu.VMEM((Z, PADDED, 128), BF16),
            pltpu.VMEM((PAIRS * LATE, 128), BF16),
            pltpu.VMEM((Z - 1, PAIRS * LATE, 128), BF16),
            pltpu.VMEM((BLOCKS - 1, BLOCK, OUT), BF16),
            pltpu.VMEM((BLOCKS, BLOCK, OUT), BF16),
            pltpu.VMEM((BLOCKS, BLOCK, 128), F32),
            pltpu.VMEM((BLOCKS, BLOCK, OUT), F32),
            dma((6,)),
            dma((2, 4, SUBS)),
            dma((2, 4, SUBS)),
            dma((Y,)),
            dma((Y,)),
            dma((2, BLOCKS - 1)),
            dma((2, BLOCKS - 1)),
            dma((2, 4, 2)),
            dma((2, 4, 2)),
            dma((Z - 1,)),
            dma((Z - 1,)),
            dma((Z - 1,)),
            dma((Z - 1,)),
            dma((Z - 1,)),
            dma((Z - 1,)),
            dma((BLOCKS - 1,)),
            dma((BLOCKS - 1,)),
        ],
        compiler_params=pltpu.CompilerParams(
            collective_id=0, has_side_effects=True, vmem_limit_bytes=60 << 20
        ),
        cost_estimate=pl.CostEstimate(
            flops=5_000_000_000, bytes_accessed=3_700_000, transcendentals=0
        ),
    )(
        token_adapter_index.reshape(1, ROWS),
        adapter_stored_row.reshape(1, -1),
        tokens,
        value_base_weight,
        adapter_down_maps.reshape(HELD, WIDTH),
        adapter_up_maps.reshape(HELD, OUT),
    )


def solution(mesh):
    return jax.shard_map(
        local,
        mesh=mesh,
        in_specs=(
            P("adapter", "tensor"),
            P("adapter"),
            P(),
            P("tensor", None),
            P("adapter", None, "tensor"),
            P("adapter", None, "tensor"),
        ),
        out_specs=P("adapter", "tensor"),
        check_vma=False,
    )
```

time: 56.9 us -> 55.5 us (0.975)
  Pallas kernels: 54.9 us -> 53.8 us
    pallas_call x1, Pallas kernels: 54.9 us -> 53.8 us  [local(): pl.pallas_call(kernel, out_shape=jax.ShapeDtypeStruct((ROWS, OUT), BF16),...]
where the time goes in v3:
time: 55.5 us; the launch traced here: 55.3 us
  Pallas kernels  53.8 us (97%)
  local copies, waits for them, and re-layouts  1.57 us (3%)
    pallas_call x1, Pallas kernels, local(): pl.pallas_call(kernel, out_shape=jax.ShapeDtypeStruct((ROWS, OUT), BF16),...  53.8 us
    unnamed x1, local copies, waits for them, and re-layouts  1.57 us

profile of v3, /device:TPU:1, one launch (start us, length us, event | category | flops | bytes accessed | tf_op | source)
XLA Modules:
  0.0 55.3 jit_solution(15342469150293468352)
XLA Ops:
  0.0 53.8 %shard_map.64 = bf16[512,128]{1,0:T(8,128)(2,1)} custom-call(s32[1,512]{1,0:T(1,128)} %bitcast.6, s32[1,128]{1,0:T(1,128)} %bitcast.7, bf16[512,1024]{1,0:T(8,128)(2,1)} %tok_hbm.1, bf16[1024,1024]{1,0:T(8,128)(2,1)} %w_hbm.1, bf16[128,1024]{1,0:T(8,128)(2,1)} %bitcast.4, bf16[128,128]{1,0:T(8,128)(2,1)} %bitcast.5), custom_call_target="tpu_custom_call" | custom-call | flops 5000000000 | bytes 3700000 | tf_op jit(solution)/shard_map/pallas_call | solution.py:453
  53.8 1.6 %copy.8 = bf16[512,128]{1,0:T(8,128)(2,1)} copy(bf16[512,128]{1,0:T(8,128)(2,1)} %shard_map.64) | data formatting | bytes 262144

commit v4 on v3

--- a/solution.py
+++ b/solution.py
@@ -199,18 +199,20 @@
         )
 
     load_tok.wait()
-    for b in (*OTHERS, 0):
-        block = dot(perm[b * BLOCK : (b + 1) * BLOCK, :], tok[...]).astype(BF16)
-        where = dot_nt(within16, perm[b * BLOCK : b * BLOCK + 128, :]).astype(BF16)
-        if b:
-            send_rows[b - 1] = block
-            send_place[b - 1] = where
-            for copy in x_copies(b):
-                copy.start()
-                slow.append(copy)
-        else:
-            rows[0] = block
-            place[0] = where
+    for dx in (1, 3, 2, 0):
+        pair = dot(perm[2 * dx * BLOCK : (2 * dx + 2) * BLOCK, :], tok[...]).astype(BF16)
+        for b in (2 * dx, 2 * dx + 1):
+            block = pair[(b - 2 * dx) * BLOCK : (b - 2 * dx + 1) * BLOCK]
+            where = dot_nt(within16, perm[b * BLOCK : b * BLOCK + 128, :]).astype(BF16)
+            if b:
+                send_rows[b - 1] = block
+                send_place[b - 1] = where
+                for copy in x_copies(b):
+                    copy.start()
+                    slow.append(copy)
+            else:
+                rows[0] = block
+                place[0] = where
 
     def product(m):
         k = lax.rem(z + m, Z)

time: 55.5 us -> 55.6 us (level)
  no operation moved by 1% of the time
where the time goes in v4:
time: 55.6 us; the launch traced here: 55.5 us
  Pallas kernels  53.9 us (97%)
  local copies, waits for them, and re-layouts  1.57 us (3%)
    pallas_call x1, Pallas kernels, local(): pl.pallas_call(kernel, out_shape=jax.ShapeDtypeStruct((ROWS, OUT), BF16),...  53.9 us
    unnamed x1, local copies, waits for them, and re-layouts  1.57 us

profile of v4, /device:TPU:1, one launch (start us, length us, event | category | flops | bytes accessed | tf_op | source)
XLA Modules:
  0.0 55.5 jit_solution(17802594598920760908)
XLA Ops:
  0.0 53.9 %shard_map.64 = bf16[512,128]{1,0:T(8,128)(2,1)} custom-call(s32[1,512]{1,0:T(1,128)} %bitcast.6, s32[1,128]{1,0:T(1,128)} %bitcast.7, bf16[512,1024]{1,0:T(8,128)(2,1)} %tok_hbm.1, bf16[1024,1024]{1,0:T(8,128)(2,1)} %w_hbm.1, bf16[128,1024]{1,0:T(8,128)(2,1)} %bitcast.4, bf16[128,128]{1,0:T(8,128)(2,1)} %bitcast.5), custom_call_target="tpu_custom_call" | custom-call | flops 5000000000 | bytes 3700000 | tf_op jit(solution)/shard_map/pallas_call | solution.py:455
  53.9 1.6 %copy.8 = bf16[512,128]{1,0:T(8,128)(2,1)} copy(bf16[512,128]{1,0:T(8,128)(2,1)} %shard_map.64) | data formatting | bytes 262144
